TPU v7x, 32 devices: a whole 2x2x4 slice. The times are simulated.
32 devices in a mesh: dp: 8 (over z, x), mp: 4 (over y, core).
Axes of the slice: x: 2, y: 2, z: 4, core: 2. Of those that a mesh axis runs over, the one named last changes fastest.
Arguments:
- states: bfloat16 [16, 1024, 768], P('dp'), may hold values from -6 to 6
- span_count: int32 [8], P('dp'), may hold values from 1 to 2, as said below
- qkv_weight: bfloat16 [768, 3, 768], P(None, None, 'mp'), may hold values from -0.21875 to 0.21875
- q_bias: float32 [768], P('mp'), may hold values from -1.5 to 1.5
- v_bias: float32 [768], P('mp'), may hold values from -1.5 to 1.5
- out_weight: bfloat16 [768, 768], P(None, 'mp'), may hold values from -3.5 to 3.5
- out_bias: float32 [768], replicated, may hold values from -1.5 to 1.5
- gain_one: float32 [768], replicated, may hold values from 0.5 to 1.5
- shift_one: float32 [768], replicated, may hold values from -1.5 to 1.5
- up_weight: bfloat16 [768, 3072], P(None, 'mp'), may hold values from -0.21875 to 0.21875
- up_bias: float32 [3072], P('mp'), may hold values from -1.5 to 1.5
- down_weight: bfloat16 [768, 3072], P(None, 'mp'), may hold values from -0.109375 to 0.109375
- down_bias: float32 [768], replicated, may hold values from -1.5 to 1.5
- gain_two: float32 [768], replicated, may hold values from 0.5 to 1.5
- shift_two: float32 [768], replicated, may hold values from -1.5 to 1.5
- cotangent: bfloat16 [16, 1024, 768], P('dp'), may hold values from -6 to 6
Outputs:
- states_out: bfloat16 [16, 1024, 768], P('dp')
- states_grad: bfloat16 [16, 1024, 768], P('dp')
- qkv_weight_grad: float32 [768, 3, 768], P(None, None, 'mp')
- q_bias_grad: float32 [768], P('mp')
- v_bias_grad: float32 [768], P('mp')
- out_weight_grad: float32 [768, 768], P(None, 'mp')
- out_bias_grad: float32 [768], replicated
- gain_one_grad: float32 [768], replicated
- shift_one_grad: float32 [768], replicated
- up_weight_grad: float32 [768, 3072], P(None, 'mp')
- up_bias_grad: float32 [3072], P('mp')
- down_weight_grad: float32 [768, 3072], P(None, 'mp')
- down_bias_grad: float32 [768], replicated
- gain_two_grad: float32 [768], replicated
- shift_two_grad: float32 [768], replicated
Inputs may be any that keep to these rules, and one draw needn't show every extreme that they name: Slots 0 to span_count[g] - 1 of dp index g hold live spans, the rest padding; some index has 2 live spans and some one.
All inputs are finite; a program needn't handle non-finite values.
Results may differ from a plain program's by a relative error of at most 0.022.
Values may be sent and summed in bfloat16 or wider, within the bound.
No kernel may reach another device: no remote copies, remote signals or barrier semaphores. Data moves between devices by JAX's collectives and lax.ppermute only.
A program may use at most 192 MiB of HBM per device.

v0:
```python
import jax
import jax.numpy as jnp
from jax import lax
from jax.sharding import PartitionSpec as P

HEAD = 64


EPS = 1e-05


def layer_norm(inputs, gain, shift):
    centre = inputs - jnp.mean(inputs, axis=-1, keepdims=True)
    spread = jnp.mean(centre * centre, axis=-1, keepdims=True)
    return centre * lax.rsqrt(spread + EPS) * gain + shift


def gelu_exact(inputs):
    return jax.nn.gelu(inputs, approximate=False)


def split_heads(matrix):
    return matrix.reshape(matrix.shape[0], matrix.shape[1] // HEAD, HEAD)


def attend_forward(queries, key_rows, values):
    query_heads = split_heads(queries)
    key_heads = split_heads(key_rows)
    value_heads = split_heads(values)
    scores = jnp.einsum(
        "qhd,khd->hqk", query_heads, key_heads, preferred_element_type=jnp.float32
    ) * HEAD ** (-0.5)
    highest = jnp.max(scores, axis=-1, keepdims=True)
    raised = jnp.exp(scores - highest)
    totals = jnp.sum(raised, axis=-1, keepdims=True)
    probabilities = (raised / totals).astype(jnp.bfloat16)
    context = jnp.einsum(
        "hqk,khd->qhd", probabilities, value_heads, preferred_element_type=jnp.float32
    )
    return (context.reshape(queries.shape[0], queries.shape[1]), highest + jnp.log(totals))


def attend_backward(queries, key_rows, values, log_total, context_grad):
    query_heads = split_heads(queries)
    key_heads = split_heads(key_rows)
    value_heads = split_heads(values)
    grad_heads = split_heads(context_grad)
    score_scale = HEAD ** (-0.5)
    scores = (
        jnp.einsum("qhd,khd->hqk", query_heads, key_heads, preferred_element_type=jnp.float32)
        * score_scale
    )
    probabilities = jnp.exp(scores - log_total)
    value_grad = jnp.einsum(
        "hqk,qhd->khd",
        probabilities.astype(jnp.bfloat16),
        grad_heads,
        preferred_element_type=jnp.float32,
    )
    prob_grad = jnp.einsum(
        "qhd,khd->hqk", grad_heads, value_heads, preferred_element_type=jnp.float32
    )
    inner = jnp.sum(prob_grad * probabilities, axis=-1, keepdims=True)
    score_grad = (probabilities * (prob_grad - inner)).astype(jnp.bfloat16)
    query_grad = (
        jnp.einsum("hqk,khd->qhd", score_grad, key_heads, preferred_element_type=jnp.float32)
        * score_scale
    )
    key_grad = (
        jnp.einsum("hqk,qhd->khd", score_grad, query_heads, preferred_element_type=jnp.float32)
        * score_scale
    )
    row_count, col_count = queries.shape
    stacked = jnp.stack(
        [
            query_grad.reshape(row_count, col_count),
            key_grad.reshape(row_count, col_count),
            value_grad.reshape(row_count, col_count),
        ]
    )
    return stacked.astype(jnp.bfloat16)


def body(
    states,
    span_count,
    qkv_weight,
    q_bias,
    v_bias,
    out_weight,
    out_bias,
    gain_one,
    shift_one,
    up_weight,
    up_bias,
    down_weight,
    down_bias,
    gain_two,
    shift_two,
    cotangent,
):
    slot_count, length, model_width = states.shape
    total_rows = slot_count * length
    live_slots = (jnp.arange(slot_count, dtype=jnp.int32) < span_count[0]).astype(jnp.float32)
    live_rows = jnp.repeat(live_slots, length)[:, None]
    flat_rows = states.reshape(total_rows, model_width)
    cot_rows = cotangent.reshape(total_rows, model_width)
    projected = jnp.einsum("rd,dtc->trc", flat_rows, qkv_weight, preferred_element_type=jnp.float32)
    queries = (projected[0] + q_bias).astype(jnp.bfloat16)
    key_rows = projected[1].astype(jnp.bfloat16)
    values = (projected[2] + v_bias).astype(jnp.bfloat16)
    contexts = []
    log_totals = []
    for slot_index in range(slot_count):
        lower = slot_index * length
        context, log_total = attend_forward(
            queries[lower : lower + length],
            key_rows[lower : lower + length],
            values[lower : lower + length],
        )
        contexts.append(context)
        log_totals.append(log_total)
    context_low = jnp.concatenate(contexts, axis=0).astype(jnp.bfloat16)
    attn_terms = jnp.einsum(
        "rc,dc->rd", context_low, out_weight, preferred_element_type=jnp.float32
    )
    attn_branch = lax.psum(attn_terms.astype(jnp.bfloat16), "mp").astype(jnp.float32) + out_bias
    first, first_pull = jax.vjp(
        layer_norm, flat_rows.astype(jnp.float32) + attn_branch, gain_one, shift_one
    )
    first_low = first.astype(jnp.bfloat16)
    hidden = jnp.dot(first_low, up_weight, preferred_element_type=jnp.float32) + up_bias
    activated, gelu_pull = jax.vjp(gelu_exact, hidden)
    act_low = activated.astype(jnp.bfloat16)
    down_terms = jnp.einsum("rf,df->rd", act_low, down_weight, preferred_element_type=jnp.float32)
    ffn_branch = lax.psum(down_terms.astype(jnp.bfloat16), "mp").astype(jnp.float32) + down_bias
    result, second_pull = jax.vjp(layer_norm, first + ffn_branch, gain_two, shift_two)
    states_out = (result * live_rows).astype(jnp.bfloat16).reshape(states.shape)
    upstream = cot_rows.astype(jnp.float32) * live_rows
    second_grad, gain_two_grad, shift_two_grad = second_pull(upstream)
    down_bias_grad = jnp.sum(second_grad, axis=0)
    branch_low = second_grad.astype(jnp.bfloat16)
    act_grad = jnp.dot(branch_low, down_weight, preferred_element_type=jnp.float32)
    down_weight_grad = jnp.einsum(
        "rd,rf->df", branch_low, act_low, preferred_element_type=jnp.float32
    )
    hidden_low = gelu_pull(act_grad)[0].astype(jnp.bfloat16)
    up_bias_grad = jnp.sum(hidden_low.astype(jnp.float32), axis=0)
    up_weight_grad = jnp.einsum(
        "rd,rf->df", first_low, hidden_low, preferred_element_type=jnp.float32
    )
    back_terms = jnp.einsum("rf,df->rd", hidden_low, up_weight, preferred_element_type=jnp.float32)
    first_grad = second_grad + lax.psum(back_terms.astype(jnp.bfloat16), "mp").astype(jnp.float32)
    entry_grad, gain_one_grad, shift_one_grad = first_pull(first_grad)
    out_bias_grad = jnp.sum(entry_grad, axis=0)
    attn_low = entry_grad.astype(jnp.bfloat16)
    context_grad = jnp.dot(attn_low, out_weight, preferred_element_type=jnp.float32).astype(
        jnp.bfloat16
    )
    out_weight_grad = jnp.einsum(
        "rd,rc->dc", attn_low, context_low, preferred_element_type=jnp.float32
    )
    slot_grads = []
    for slot_index in range(slot_count):
        lower = slot_index * length
        slot_grads.append(
            attend_backward(
                queries[lower : lower + length],
                key_rows[lower : lower + length],
                values[lower : lower + length],
                log_totals[slot_index],
                context_grad[lower : lower + length],
            )
        )
    proj_low = jnp.concatenate(slot_grads, axis=1)
    qkv_weight_grad = jnp.einsum(
        "rd,trc->dtc", flat_rows, proj_low, preferred_element_type=jnp.float32
    )
    q_bias_grad = jnp.sum(proj_low[0].astype(jnp.float32), axis=0)
    v_bias_grad = jnp.sum(proj_low[2].astype(jnp.float32), axis=0)
    input_terms = jnp.einsum(
        "trc,dtc->rd", proj_low, qkv_weight, preferred_element_type=jnp.float32
    )
    states_grad = (
        (entry_grad + lax.psum(input_terms.astype(jnp.bfloat16), "mp").astype(jnp.float32))
        .astype(jnp.bfloat16)
        .reshape(states.shape)
    )
    (
        qkv_share,
        q_bias_share,
        v_bias_share,
        out_weight_share,
        out_bias_share,
        gain_one_share,
        shift_one_share,
        up_weight_share,
        up_bias_share,
        down_weight_share,
        down_bias_share,
        gain_two_share,
        shift_two_share,
    ) = (
        lax.psum_scatter(qkv_weight_grad, "dp", scatter_dimension=0, tiled=True),
        lax.psum_scatter(q_bias_grad, "dp", scatter_dimension=0, tiled=True),
        lax.psum_scatter(v_bias_grad, "dp", scatter_dimension=0, tiled=True),
        lax.psum_scatter(out_weight_grad, "dp", scatter_dimension=0, tiled=True),
        lax.psum_scatter(out_bias_grad, "dp", scatter_dimension=0, tiled=True),
        lax.psum_scatter(gain_one_grad, "dp", scatter_dimension=0, tiled=True),
        lax.psum_scatter(shift_one_grad, "dp", scatter_dimension=0, tiled=True),
        lax.psum_scatter(up_weight_grad, "dp", scatter_dimension=0, tiled=True),
        lax.psum_scatter(up_bias_grad, "dp", scatter_dimension=0, tiled=True),
        lax.psum_scatter(down_weight_grad, "dp", scatter_dimension=0, tiled=True),
        lax.psum_scatter(down_bias_grad, "dp", scatter_dimension=0, tiled=True),
        lax.psum_scatter(gain_two_grad, "dp", scatter_dimension=0, tiled=True),
        lax.psum_scatter(shift_two_grad, "dp", scatter_dimension=0, tiled=True),
    )
    gathered = (
        lax.all_gather(qkv_share.astype(jnp.bfloat16), "dp", axis=0, tiled=True).astype(
            qkv_share.dtype
        ),
        lax.all_gather(q_bias_share.astype(jnp.bfloat16), "dp", axis=0, tiled=True).astype(
            q_bias_share.dtype
        ),
        lax.all_gather(v_bias_share.astype(jnp.bfloat16), "dp", axis=0, tiled=True).astype(
            v_bias_share.dtype
        ),
        lax.all_gather(out_weight_share.astype(jnp.bfloat16), "dp", axis=0, tiled=True).astype(
            out_weight_share.dtype
        ),
        lax.all_gather(out_bias_share.astype(jnp.bfloat16), "dp", axis=0, tiled=True).astype(
            out_bias_share.dtype
        ),
        lax.all_gather(gain_one_share.astype(jnp.bfloat16), "dp", axis=0, tiled=True).astype(
            gain_one_share.dtype
        ),
        lax.all_gather(shift_one_share.astype(jnp.bfloat16), "dp", axis=0, tiled=True).astype(
            shift_one_share.dtype
        ),
        lax.all_gather(up_weight_share.astype(jnp.bfloat16), "dp", axis=0, tiled=True).astype(
            up_weight_share.dtype
        ),
        lax.all_gather(up_bias_share.astype(jnp.bfloat16), "dp", axis=0, tiled=True).astype(
            up_bias_share.dtype
        ),
        lax.all_gather(down_weight_share.astype(jnp.bfloat16), "dp", axis=0, tiled=True).astype(
            down_weight_share.dtype
        ),
        lax.all_gather(down_bias_share.astype(jnp.bfloat16), "dp", axis=0, tiled=True).astype(
            down_bias_share.dtype
        ),
        lax.all_gather(gain_two_share.astype(jnp.bfloat16), "dp", axis=0, tiled=True).astype(
            gain_two_share.dtype
        ),
        lax.all_gather(shift_two_share.astype(jnp.bfloat16), "dp", axis=0, tiled=True).astype(
            shift_two_share.dtype
        ),
    )
    return (
        states_out,
        states_grad,
        gathered[0],
        gathered[1],
        gathered[2],
        gathered[3],
        gathered[4],
        gathered[5],
        gathered[6],
        gathered[7],
        gathered[8],
        gathered[9],
        gathered[10],
        gathered[11],
        gathered[12],
    )


def solution(mesh):
    in_specs = (
        P("dp", None, None),
        P("dp"),
        P(None, None, "mp"),
        P("mp"),
        P("mp"),
        P(None, "mp"),
        P(),
        P(),
        P(),
        P(None, "mp"),
        P("mp"),
        P(None, "mp"),
        P(),
        P(),
        P(),
        P("dp", None, None),
    )
    out_specs = (
        P("dp", None, None),
        P("dp", None, None),
        P(None, None, "mp"),
        P("mp"),
        P("mp"),
        P(None, "mp"),
        P(),
        P(),
        P(),
        P(None, "mp"),
        P("mp"),
        P(None, "mp"),
        P(),
        P(),
        P(),
    )
    return jax.shard_map(body, mesh=mesh, in_specs=in_specs, out_specs=out_specs, check_vma=False)
```

profile of v0, /device:TPU:0, one launch (start us, length us, event | category | flops | bytes accessed | tf_op | source)
XLA Modules:
  0.0 752.4 jit_solution(4771210637834142543)
XLA Ops:
  33.2 71.2 %all-reduce.25.cloned.1.call-done = bf16[2048,768]{1,0:T(8,128)(2,1)} async-done(((bf16[2048,768]{1,0:T(8,128)(2,1)}), bf16[2048,768]{1,0:T(8,128)(2,1)}) %all-reduce.25.cloned.1.call-update) | async-done | bytes 3145744 | tf_op jit(solution)/shard_map/psum | solution.py:127
  111.6 18.0 %multiply_convert_fusion.3 = (bf16[2048,768]{1,0:T(8,128)(2,1)S(1)}, f32[2048,768]{1,0:T(8,128)}, f32[2048,768]{1,0:T(8,128)}) fusion(f32[768]{0:T(1024)S(1)} %copy-done.44, bf16[768,768]{1,0:T(8,128)(2,1)S(1)} %copy-done, f32[2048,768]{1,0:T(8,128)S(1)} %get-tuple-element.80, f32[768]{0:T(1024)S(1)} %copy-done.36, f32[768]{0:T(1024)S(1)} %copy-done.32, ...), kind=kOutput, calls=%fused_computation.34 | convolution fusion | flops 2526019584 | bytes 23217152 | tf_op jit(solution)/shard_map/dot_general | solution.py:132
  136.1 67.9 %all-reduce.27.cloned.1.call-done = bf16[2048,768]{1,0:T(8,128)(2,1)} async-done(((bf16[2048,768]{1,0:T(8,128)(2,1)}), bf16[2048,768]{1,0:T(8,128)(2,1)}) %all-reduce.27.cloned.1.call-update) | async-done | bytes 3145744 | tf_op jit(solution)/shard_map/psum | solution.py:136
  229.0 8.0 %fusion.45 = f32[768,768]{1,0:T(8,128)} fusion(bf16[2048,768]{1,0:T(8,128)(2,1)} %copy-done.46, f32[2048,768]{1,0:T(8,128)} %copy-done.5, f32[2048]{0:T(1024)S(1)} %negate_multiply_fusion.2), kind=kOutput, calls=%fused_computation.121 | convolution fusion | flops 2419064832 | bytes 11804672 | tf_op jit(solution)/shard_map/rd,rf->df/dot_general | solution.py:144
  237.1 8.0 %fusion.48 = f32[768,768]{1,0:T(8,128)} fusion(bf16[2048,768]{1,0:T(8,128)(2,1)} %copy-done.45, f32[2048,768]{1,0:T(8,128)} %copy-done.4, f32[768]{0:T(1024)S(1)} %copy-done.36, f32[768]{0:T(1024)S(1)} %copy-done.32, f32[2048]{0:T(1024)S(1)} %fusion.37), kind=kOutput, calls=%fused_computation.124 | convolution fusion | flops 2422210560 | bytes 11810816 | tf_op jit(solution)/shard_map/rd,rf->df/dot_general | solution.py:149
  245.2 52.3 %all-reduce.29.cloned.1.call-done = bf16[2048,768]{1,0:T(8,128)(2,1)} async-done(((bf16[2048,768]{1,0:T(8,128)(2,1)}), bf16[2048,768]{1,0:T(8,128)(2,1)}) %all-reduce.29.cloned.1.call-update) | async-done | bytes 3145744 | tf_op jit(solution)/shard_map/psum | solution.py:153
  297.5 7.2 multiply_reduce_fusion.6
  304.7 6.4 fusion.53
  319.2 5.6 multiply_convert_fusion.1
  324.8 5.0 fusion.25
  333.9 7.1 fusion.28
  341.0 7.1 fusion.31
  348.1 6.2 multiply_reduce_fusion
  354.4 10.1 %multiply_convert_fusion = bf16[3,1024,1024]{1,2,0:T(8,128)(2,1)S(1)} fusion(f32[3,1024,1024]{1,2,0:T(8,128)} %get-tuple-element.104, f32[3,1024,1024]{1,2,0:T(8,128)} %copy-done.2, f32[3,1024]{1,0:T(4,128)S(1)} %get-tuple-element.103, f32[3,1024]{1,0:T(4,128)S(1)} %log_add_fusion), kind=kLoop, calls=%fused_computation | loop fusion | flops 15728640 | bytes 31481856 | tf_op jit(solution)/shard_map/convert_element_type | solution.py:64
  367.9 4.9 bitcast_convert_fusion
  380.9 61.7 %reduce-scatter.9.cloned.1.call-done = f32[96,768]{1,0:T(8,128)} async-done(((f32[768,768]{1,0:T(8,128)}), f32[96,768]{1,0:T(8,128)}) %reduce-scatter.9.cloned.1.call-update) | async-done | bytes 294928 | tf_op jit(solution)/shard_map/reduce_scatter | solution.py:211
  450.6 57.2 %reduce-scatter.7.cloned.1.call-done = f32[96,192]{1,0:T(8,128)} async-done(((f32[768,192]{1,0:T(8,128)}), f32[96,192]{1,0:T(8,128)}) %reduce-scatter.7.cloned.1.call-update) | async-done | bytes 73744 | tf_op jit(solution)/shard_map/reduce_scatter | solution.py:207
  508.7 31.2 %all_gather.42 = bf16[768,192]{1,0:T(8,128)(2,1)S(1)} all-gather(bf16[96,192]{1,0:T(8,128)(2,1)S(1)} %convert_element_type.217), channel_id=1, replica_groups=mesh['dp'=8,'mp'=4] {'dp'}, dimensions={0}, use_global_device_ids=true | all-gather | bytes 331776 | tf_op jit(solution)/shard_map/all_gather | solution.py:228
  540.9 37.4 %all-reduce.31.cloned.1.call-done = bf16[2048,768]{1,0:T(8,128)(2,1)} async-done(((bf16[2048,768]{1,0:T(8,128)(2,1)}), bf16[2048,768]{1,0:T(8,128)(2,1)}) %all-reduce.31.cloned.1.call-update) | async-done | bytes 3145744 | tf_op jit(solution)/shard_map/psum | solution.py:185
  578.3 5.4 add_reduce_fusion
  583.7 38.0 %all-reduce.18 = (bf16[192]{0:T(256)(128)(2,1)S(1)}, bf16[192]{0:T(256)(128)(2,1)S(1)}, bf16[768]{0:T(1024)(128)(2,1)S(1)}, bf16[768]{0:T(1024)(128)(2,1)S(1)}, ...) all-reduce(f32[192]{0:T(256)S(1)} %get-tuple-element.52, ...), channel_id=3, replica_groups=mesh['dp'=8,'mp'=4] {'dp'}, use_global_device_ids=true, to_apply=%region_20.0.clone | all-reduce | flops 5760 | bytes 34560
  624.2 33.3 %all-reduce.19 = (bf16[192]{0:T(256)(128)(2,1)S(1)}, bf16[192]{0:T(256)(128)(2,1)S(1)}, bf16[768]{0:T(1024)(128)(2,1)S(1)}, bf16[768]{0:T(1024)(128)(2,1)S(1)}, ...) all-reduce(bf16[192]{0:T(256)(128)(2,1)S(1)} %dynamic-update-slice,, ...), channel_id=1, replica_groups=mesh['dp'=8,'mp'=4] {'dp'}, use_global_device_ids=true, to_apply=%add | all-reduce | flops 5760 | bytes 23040
  664.2 35.6 %all_gather.39 = bf16[768,3,192]{2,1,0:T(4,128)(2,1)S(1)} all-gather(bf16[96,3,192]{2,1,0:T(4,128)(2,1)S(1)} %copy.48), channel_id=1, replica_groups=mesh['dp'=8,'mp'=4] {'dp'}, dimensions={0}, use_global_device_ids=true | all-gather | bytes 995328 | tf_op jit(solution)/shard_map/all_gather | solution.py:219
  704.8 37.3 %all-gather.3.cloned.1.call-done = bf16[768,768]{1,0:T(8,128)(2,1)} async-done(((bf16[96,768]{1,0:T(8,128)(2,1)}), bf16[768,768]{1,0:T(8,128)(2,1)}) %all-gather.3.cloned.1.call-update) | async-done | bytes 1179664 | tf_op jit(solution)/shard_map/all_gather | solution.py:240
  (231 shorter events, 111.3 us)
Async XLA Ops:
  7.2 104.4 %copy-start = (bf16[768,768]{1,0:T(8,128)(2,1)S(1)}, bf16[768,768]{1,0:T(8,128)(2,1)}, u32[]{:S(2)}) copy-start(bf16[768,768]{1,0:T(8,128)(2,1)} %param.25) | copy-start | bytes 3538948
  7.2 97.2 %all-reduce.25.cloned.1.call-start = ((), (), s32[]{:S(2)}) async-start(), calls=%async_computation.4 | async-start | bytes 6291456 | tf_op jit(solution)/shard_map/psum | solution.py:127
  30.4 74.0 %copy-start.33 = (f32[768]{0:T(1024)S(1)}, f32[768]{0:T(1024)}, u32[]{:S(2)}) copy-start(f32[768]{0:T(1024)} %param.22) | copy-start | bytes 9220
  33.1 170.9 %all-reduce.27.cloned.1.call-start = ((), (), s32[]{:S(2)}) async-start(), calls=%async_computation.5 | async-start | bytes 6291456 | tf_op jit(solution)/shard_map/psum | solution.py:136
  111.6 18.1 %copy-start.4 = (f32[2048,768]{1,0:T(8,128)}, f32[2048,768]{1,0:T(8,128)S(1)}, u32[]{:S(2)}) copy-start(f32[2048,768]{1,0:T(8,128)S(1)} %get-tuple-element.80) | copy-start | bytes 18874372
  111.6 19.6 %copy-start.41 = (bf16[768,768]{1,0:T(8,128)(2,1)S(1)}, bf16[768,768]{1,0:T(8,128)(2,1)}, u32[]{:S(2)}) copy-start(bf16[768,768]{1,0:T(8,128)(2,1)} %param.27) | copy-start | bytes 3538948
  131.3 72.7 %copy-start.35 = (f32[768]{0:T(1024)S(1)}, f32[768]{0:T(1024)}, u32[]{:S(2)}) copy-start(f32[768]{0:T(1024)} %param.28) | copy-start | bytes 9220
  135.3 162.2 %all-reduce.29.cloned.1.call-start = ((), (), s32[]{:S(2)}) async-start(), calls=%async_computation.6 | async-start | bytes 6291456 | tf_op jit(solution)/shard_map/psum | solution.py:153
  228.8 150.3 %reduce-scatter.11.cloned.1.call-start = ((), (), s32[]{:S(2)}) async-start(), calls=%async_computation.11 | async-start | bytes 2654208 | tf_op jit(solution)/shard_map/reduce_scatter | solution.py:213
  237.0 205.5 %reduce-scatter.9.cloned.1.call-start = ((), (), s32[]{:S(2)}) async-start(), calls=%async_computation.9 | async-start | bytes 2654208 | tf_op jit(solution)/shard_map/reduce_scatter | solution.py:211
  245.1 262.7 %reduce-scatter.7.cloned.1.call-start = ((), (), s32[]{:S(2)}) async-start(), calls=%async_computation.8 | async-start | bytes 884736 | tf_op jit(solution)/shard_map/reduce_scatter | solution.py:207
  329.8 38.0 %copy-start.23 = (bf16[3,64,1024]{2,1,0:T(8,128)(2,1)}, bf16[3,64,1024]{2,1,0:T(8,128)(2,1)S(1)}, u32[]{:S(2)}) copy-start(bf16[3,64,1024]{2,1,0:T(8,128)(2,1)S(1)} %fusion.25) | copy-start | bytes 1179652
  331.5 36.4 %copy-start.25 = (bf16[3,64,1024]{2,1,0:T(8,128)(2,1)}, bf16[3,64,1024]{2,1,0:T(8,128)(2,1)S(1)}, u32[]{:S(2)}) copy-start(bf16[3,64,1024]{2,1,0:T(8,128)(2,1)S(1)} %fusion.24) | copy-start | bytes 1179652
  333.9 14.2 %slice-start.1 = ((s8[12582912]{0:T(1024)(128)(4,1)}), s8[4194304]{0:T(1024)(128)(4,1)S(1)}, s32[]{:S(2)}) async-start(s8[12582912]{0:T(1024)(128)(4,1)} %bitcast.116), calls=%async_computation.15 | async-start | bytes 8388608
  354.4 223.9 %all-reduce.31.cloned.1.call-start = ((), (), s32[]{:S(2)}) async-start(), calls=%async_computation.7 | async-start | bytes 6291456 | tf_op jit(solution)/shard_map/psum | solution.py:185
  372.9 290.0 %reduce-scatter.13.cloned.1.call-start = ((), (), s32[]{:S(2)}) async-start(), calls=%async_computation.13 | async-start | bytes 2211840
  377.2 67.1 %copy-start.38 = (u32[32]{0:T(128)S(1)}, u32[32]{0:T(128)}, u32[]{:S(2)}) copy-start(u32[32]{0:T(128)} %constant.87) | copy-start | bytes 388
  377.2 73.1 %copy-start.24 = (bf16[3,64,1024]{2,1,0:T(8,128)(2,1)S(1)}, bf16[3,64,1024]{2,1,0:T(8,128)(2,1)}, u32[]{:S(2)}) copy-start(bf16[3,64,1024]{2,1,0:T(8,128)(2,1)} %copy-done.23) | copy-start | bytes 1179652
  377.2 73.1 %copy-start.26 = (bf16[3,64,1024]{2,1,0:T(8,128)(2,1)S(1)}, bf16[3,64,1024]{2,1,0:T(8,128)(2,1)}, u32[]{:S(2)}) copy-start(bf16[3,64,1024]{2,1,0:T(8,128)(2,1)} %copy-done.25) | copy-start | bytes 1179652
  379.0 71.3 %copy-start.28 = (bf16[3,64,1024]{2,1,0:T(8,128)(2,1)S(1)}, bf16[3,64,1024]{2,1,0:T(8,128)(2,1)}, u32[]{:S(2)}) copy-start(bf16[3,64,1024]{2,1,0:T(8,128)(2,1)} %copy-done.27) | copy-start | bytes 1179652
  379.0 71.3 %copy-start.30 = (bf16[3,64,1024]{2,1,0:T(8,128)(2,1)S(1)}, bf16[3,64,1024]{2,1,0:T(8,128)(2,1)}, u32[]{:S(2)}) copy-start(bf16[3,64,1024]{2,1,0:T(8,128)(2,1)} %copy-done.29) | copy-start | bytes 1179652
  379.0 323.0 %all-gather.5.cloned.1.call-start = ((), (), s32[]{:S(2)}) async-start(), calls=%async_computation.12 | async-start | bytes 1327104 | tf_op jit(solution)/shard_map/all_gather | solution.py:246
  380.8 361.4 %all-gather.3.cloned.1.call-start = ((), (), s32[]{:S(2)}) async-start(), calls=%async_computation.10 | async-start | bytes 1327104 | tf_op jit(solution)/shard_map/all_gather | solution.py:240
  662.8 82.2 %copy-start.1 = (bf16[768,768]{1,0:T(8,128)(2,1)S(1)}, bf16[768,768]{1,0:T(8,128)(2,1)}, u32[]{:S(2)}) copy-start(bf16[768,768]{1,0:T(8,128)(2,1)} %param.25) | copy-start | bytes 3538948
  (43 other events, 232.9 us)
Sparse Core Ops, SparseCore 0:
  33.2 71.1 all-reduce.24
  135.4 68.5 all-reduce.26
  228.9 68.5 all-reduce.28
  301.4 69.0 reduce-scatter.10
  374.5 68.0 reduce-scatter.8
  446.3 61.4 reduce-scatter.6
  510.9 67.4 all-reduce.30
  582.2 66.7 reduce-scatter.12
  651.2 48.2 all-gather.4
  702.0 40.0 all-gather.2
where the time goes:
time: 757 us; the launch traced here: 752 us
  waiting for transfers between devices  385 us (51%)
  blocking collectives  138 us (18%)
  matrix products  109 us (14%)
  other arithmetic  76.9 us (10%)
  local copies, waits for them, and re-layouts  23.1 us (3%)
  between operations  18.9 us (2%)
    unnamed x2, blocking collectives  71.3 us
    psum x1, waiting for transfers between devices, body(): lax.psum(attn_terms.astype(jnp.bfloat16), 'mp').astype(jnp.float32)  71.2 us
    psum x1, waiting for transfers between devices, body(): lax.psum(down_terms.astype(jnp.bfloat16), 'mp').astype(jnp.float32)  67.9 us
    reduce_scatter x1, waiting for transfers between devices, body(): lax.psum_scatter(up_weight_grad, 'dp', scatter_dimension=0, tiled=True)  61.7 us
    reduce_scatter x1, waiting for transfers between devices, body(): lax.psum_scatter(out_weight_grad, 'dp', scatter_dimension=0, tiled=True)  57.2 us
    psum x1, waiting for transfers between devices, body(): lax.psum(back_terms.astype(jnp.bfloat16), 'mp').astype(jnp.float32)  52.3 us
    psum x1, waiting for transfers between devices, body(): lax.psum(input_terms.astype(jnp.bfloat16), 'mp').astype(jnp.float32)  37.4 us
    all_gather x1, waiting for transfers between devices, body(): lax.all_gather(up_weight_share.astype(jnp.bfloat16), 'dp', axis=0, tiled=...  37.3 us
  transfers between devices with their start and end apart: 10, of which 7 were waited for; matrix products, arithmetic and copies ran while one was open for 16% of the time, Pallas kernels for 0%

commit v1 on v0

v1 whole, which is shorter than its diff:
```python
import jax
import jax.numpy as jnp
from jax import lax
from jax.sharding import PartitionSpec as P

HEAD = 64
EPS = 1e-05
F32 = jnp.float32
BF16 = jnp.bfloat16
CORE, ROW, SIDE = 1, 2, 4


def norm_forward(inputs):
    centre = inputs - jnp.mean(inputs, axis=-1, keepdims=True)
    spread = jnp.mean(centre * centre, axis=-1, keepdims=True)
    scale = lax.rsqrt(spread + EPS)
    return centre * scale, scale


def norm_backward(grad, normed, scale, gain):
    scaled = grad * gain
    mean_one = jnp.mean(scaled, axis=-1, keepdims=True)
    mean_two = jnp.mean(scaled * normed, axis=-1, keepdims=True)
    return scale * (scaled - mean_one - normed * mean_two)


def split_heads(matrix):
    return matrix.reshape(matrix.shape[0], matrix.shape[1] // HEAD, HEAD)


def attend_forward(rows, weight, q_bias, v_bias):
    projected = jnp.einsum("rd,dtc->trc", rows, weight, preferred_element_type=F32)
    queries = (projected[0] + q_bias).astype(BF16)
    key_rows = projected[1].astype(BF16)
    values = (projected[2] + v_bias).astype(BF16)
    scores = jnp.einsum("qhd,khd->hqk", split_heads(queries), split_heads(key_rows), preferred_element_type=F32) * HEAD**-0.5
    highest = jnp.max(scores, axis=-1, keepdims=True)
    raised = jnp.exp(scores - highest)
    totals = jnp.sum(raised, axis=-1, keepdims=True)
    probabilities = (raised / totals).astype(BF16)
    context = jnp.einsum("hqk,khd->qhd", probabilities, split_heads(values), preferred_element_type=F32)
    return queries, key_rows, values, context.reshape(queries.shape).astype(BF16), highest + jnp.log(totals)


def attend_backward(kept, context_grad):
    queries, key_rows, values, _, log_total = kept
    query_heads, key_heads, value_heads, grad_heads = map(split_heads, (queries, key_rows, values, context_grad))
    scores = jnp.einsum("qhd,khd->hqk", query_heads, key_heads, preferred_element_type=F32) * HEAD**-0.5
    probabilities = jnp.exp(scores - log_total)
    value_grad = jnp.einsum("hqk,qhd->khd", probabilities.astype(BF16), grad_heads, preferred_element_type=F32)
    prob_grad = jnp.einsum("qhd,khd->hqk", grad_heads, value_heads, preferred_element_type=F32)
    inner = jnp.sum(prob_grad * probabilities, axis=-1, keepdims=True)
    score_grad = (probabilities * (prob_grad - inner)).astype(BF16)
    query_grad = jnp.einsum("hqk,khd->qhd", score_grad, key_heads, preferred_element_type=F32) * HEAD**-0.5
    key_grad = jnp.einsum("hqk,qhd->khd", score_grad, query_heads, preferred_element_type=F32) * HEAD**-0.5
    return jnp.stack([g.reshape(queries.shape) for g in (query_grad, key_grad, value_grad)]).astype(BF16)


def build(mesh):
    n_dp, n_mp = mesh.shape["dp"], mesh.shape["mp"]
    dp_flips = []
    step = n_mp
    while step < n_dp * n_mp:
        dp_flips.append(step)
        step *= 2

    def flip(value, bit):
        pairs = [(i, i ^ bit) for i in range(n_dp * n_mp)]
        return lax.ppermute(value, ("dp", "mp"), pairs)

    def body(
        states, span_count, qkv_weight, q_bias, v_bias, out_weight, out_bias, gain_one, shift_one,
        up_weight, up_bias, down_weight, down_bias, gain_two, shift_two, cotangent,
    ):
        place = lax.axis_index("dp") * n_mp + lax.axis_index("mp")
        slot = (place // ROW) % 2
        core = place % 2

        def half(value, bit, mine):
            which = (place // bit) % 2
            which = which if mine else 1 - which
            size = value.shape[0] // 2
            return lax.dynamic_slice_in_dim(value, which * size, size, 0)

        def join(value, bit):
            other = flip(value, bit)
            first = (place // bit) % 2 == 0
            return jnp.concatenate([jnp.where(first, value, other), jnp.where(first, other, value)], axis=0)

        def total_dp(value):
            for bit in dp_flips:
                value = (half(value, bit, True).astype(F32) + flip(half(value, bit, False), bit).astype(F32)).astype(BF16)
            for bit in reversed(dp_flips):
                value = join(value, bit)
            return value

        def total_group(own, other):
            own = (own.astype(F32) + flip(other, ROW).astype(F32)).astype(BF16)
            return total_dp(own).astype(F32)

        def total_small(value):
            for bit in dp_flips:
                value = value + flip(value, bit)
            return value

        rows = lax.dynamic_index_in_dim(states, slot, 0, False)
        cot = lax.dynamic_index_in_dim(cotangent, slot, 0, False)
        live = (slot < span_count[0]).astype(F32)
        q_bias_o, v_bias_o, up_bias_o = jnp.split(flip(jnp.concatenate([q_bias, v_bias, up_bias]), ROW), [192, 384])
        qkv_o = flip(qkv_weight, ROW)
        out_o = flip(out_weight, ROW)
        up_o = flip(up_weight, ROW)
        down_o = flip(down_weight, ROW)

        kept = attend_forward(rows, qkv_weight, q_bias, v_bias)
        kept_o = attend_forward(rows, qkv_o, q_bias_o, v_bias_o)
        context = jnp.concatenate([kept[3], kept_o[3]], axis=1)
        out_both = jnp.concatenate([out_weight, out_o], axis=1)
        terms = jnp.einsum("rc,dc->rd", context, out_both, preferred_element_type=F32).astype(BF16)
        attn_branch = terms.astype(F32) + flip(terms, CORE).astype(F32) + out_bias
        normed_one, scale_one = norm_forward(rows.astype(F32) + attn_branch)
        first = normed_one * gain_one + shift_one
        first_low = first.astype(BF16)
        up_both = jnp.concatenate([up_weight, up_o], axis=1)
        down_both = jnp.concatenate([down_weight, down_o], axis=1)
        hidden = jnp.dot(first_low, up_both, preferred_element_type=F32) + jnp.concatenate([up_bias, up_bias_o])
        activated, gelu_pull = jax.vjp(lambda h: jax.nn.gelu(h, approximate=False), hidden)
        act_low = activated.astype(BF16)
        terms = jnp.einsum("rf,df->rd", act_low, down_both, preferred_element_type=F32).astype(BF16)
        ffn_branch = terms.astype(F32) + flip(terms, CORE).astype(F32) + down_bias
        normed_two, scale_two = norm_forward(first + ffn_branch)
        out_rows = ((normed_two * gain_two + shift_two) * live).astype(BF16)

        def share_rows(span):
            other = join(flip(half(span, CORE, True), ROW), CORE)
            lower = slot == 0
            return jnp.stack([jnp.where(lower, span, other), jnp.where(lower, other, span)])

        states_out = share_rows(out_rows)
        upstream = cot.astype(F32) * live
        gain_two_grad = jnp.sum(upstream * normed_two, axis=0)
        shift_two_grad = jnp.sum(upstream, axis=0)
        second_grad = norm_backward(upstream, normed_two, scale_two, gain_two)
        down_bias_grad = jnp.sum(second_grad, axis=0)
        branch_low = second_grad.astype(BF16)
        act_grad = jnp.dot(branch_low, down_both, preferred_element_type=F32)
        down_grad = jnp.einsum("rd,rf->df", branch_low, act_low, preferred_element_type=F32).astype(BF16)
        hidden_low = gelu_pull(act_grad)[0].astype(BF16)
        up_bias_both = jnp.sum(hidden_low.astype(F32), axis=0)
        up_grad = jnp.einsum("rd,rf->df", first_low, hidden_low, preferred_element_type=F32).astype(BF16)
        terms = jnp.einsum("rf,df->rd", hidden_low, up_both, preferred_element_type=F32).astype(BF16)
        first_grad = second_grad + (terms.astype(F32) + flip(terms, CORE).astype(F32))
        gain_one_grad = jnp.sum(first_grad * normed_one, axis=0)
        shift_one_grad = jnp.sum(first_grad, axis=0)
        entry_grad = norm_backward(first_grad, normed_one, scale_one, gain_one)
        out_bias_grad = jnp.sum(entry_grad, axis=0)
        attn_low = entry_grad.astype(BF16)
        context_grad = jnp.dot(attn_low, out_both, preferred_element_type=F32).astype(BF16)
        out_grad = jnp.einsum("rd,rc->dc", attn_low, context, preferred_element_type=F32).astype(BF16)
        proj = attend_backward(kept, context_grad[:, :192])
        proj_o = attend_backward(kept_o, context_grad[:, 192:])
        qkv_grad = jnp.einsum("rd,trc->dtc", rows, proj, preferred_element_type=F32).astype(BF16)
        qkv_grad_o = jnp.einsum("rd,trc->dtc", rows, proj_o, preferred_element_type=F32).astype(BF16)
        terms = jnp.einsum("trc,dtc->rd", proj, qkv_weight, preferred_element_type=F32)
        terms = (terms + jnp.einsum("trc,dtc->rd", proj_o, qkv_o, preferred_element_type=F32)).astype(BF16)
        in_rows = (entry_grad + (terms.astype(F32) + flip(terms, CORE).astype(F32))).astype(BF16)
        states_grad = share_rows(in_rows)

        ff = up_weight.shape[1]
        down_total = total_group(down_grad[:, :ff], down_grad[:, ff:])
        up_total = total_group(up_grad[:, :ff], up_grad[:, ff:])
        out_total = total_group(out_grad[:, :192], out_grad[:, 192:])
        qkv_total = total_group(qkv_grad, qkv_grad_o)
        common = [out_bias_grad, gain_one_grad, shift_one_grad, down_bias_grad, gain_two_grad, shift_two_grad]
        width = common[0].shape[0]
        bias = lambda p: [jnp.sum(p[0].astype(F32), axis=0), jnp.sum(p[2].astype(F32), axis=0)]
        mine = jnp.concatenate(common + [up_bias_both[:ff]] + bias(proj))
        theirs = jnp.concatenate(common + [up_bias_both[ff:]] + bias(proj_o))
        small = total_small(mine + flip(theirs, ROW))
        small = small.astype(BF16).astype(F32)
        parts = jnp.split(small, [width * i for i in range(1, 7)] + [6 * width + ff, 6 * width + ff + 192])
        return (
            states_out, states_grad, qkv_total, parts[7], parts[8], out_total, parts[0], parts[1], parts[2],
            up_total, parts[6], down_total, parts[3], parts[4], parts[5],
        )

    return body


def solution(mesh):
    split = P("dp", None, None)
    in_specs = (
        split, P("dp"), P(None, None, "mp"), P("mp"), P("mp"), P(None, "mp"), P(), P(), P(),
        P(None, "mp"), P("mp"), P(None, "mp"), P(), P(), P(), split,
    )
    out_specs = (
        split, split, P(None, None, "mp"), P("mp"), P("mp"), P(None, "mp"), P(), P(), P(),
        P(None, "mp"), P("mp"), P(None, "mp"), P(), P(), P(),
    )
    return jax.shard_map(build(mesh), mesh=mesh, in_specs=in_specs, out_specs=out_specs, check_vma=False)
```

time: 757 us -> 423 us (0.56)
  waiting for transfers between devices: 385 us -> 183 us
  blocking collectives: 138 us -> 0 us
  starting transfers between devices: 0.59 us -> 41.5 us
  between operations: 18.9 us -> 3.49 us
  matrix products: 109 us -> 94.5 us
    psum x4 -> x0, waiting for transfers between devices: 229 us -> none  [the longest x1 71.2 us: body(): lax.psum(attn_terms.astype(jnp.bfloat16), 'mp').astype(jnp.float32)]
    ppermute x0 -> x45, waiting for transfers between devices: none -> 183 us  [flip(): return lax.ppermute(value, ('dp', 'mp'), pairs)]
    reduce_scatter x3 -> x0, waiting for transfers between devices: 119 us -> none  [the longest x1 61.7 us: body(): lax.psum_scatter(up_weight_grad, 'dp', scatter_dimension=0, tiled=True)]
    unnamed x2 -> x0, blocking collectives: 71.3 us -> none
    all_gather x2 -> x0, blocking collectives: 66.8 us -> none  [the longest x1 35.6 us: body(): lax.all_gather(qkv_share.astype(jnp.bfloat16), 'dp', axis=0, tiled=True)]
    ppermute x0 -> x45, starting transfers between devices: none -> 41.5 us  [flip(): return lax.ppermute(value, ('dp', 'mp'), pairs)]
    all_gather x2 -> x0, waiting for transfers between devices: 37.3 us -> none  [the longest x1 37.3 us: body(): lax.all_gather(up_weight_share.astype(jnp.bfloat16), 'dp', axis=0, tiled=...]
    dot_general x18 -> x17, matrix products: 90.1 us -> 63 us  [the longest x1 17.6 us: body(): jnp.dot(first_low, up_both, preferred_element_type=F32)]
  transfers between devices with their start and end apart: 10 -> 45, of which waited for: 7 -> 24; matrix products, arithmetic and copies ran while one was open for 16% -> 31% of each run, Pallas kernels for 0% -> 0%
where the time goes in v1:
time: 423 us; the launch traced here: 418 us
  waiting for transfers between devices  183 us (43%)
  matrix products  94.5 us (22%)
  other arithmetic  70.9 us (17%)
  starting transfers between devices  41.5 us (10%)
  local copies, waits for them, and re-layouts  24.1 us (6%)
    ppermute x45, waiting for transfers between devices, flip(): return lax.ppermute(value, ('dp', 'mp'), pairs)  183 us
    ppermute x45, starting transfers between devices, flip(): return lax.ppermute(value, ('dp', 'mp'), pairs)  41.5 us
    convert_element_type x2, other arithmetic, attend_backward(): score_grad = (probabilities * (prob_grad - inner)).astype(BF16)  20.1 us
    dot_general x1, matrix products, body(): jnp.dot(first_low, up_both, preferred_element_type=F32)  17.6 us
    dot_general x2, matrix products, attend_backward(): jnp.einsum('qhd,khd->hqk', grad_heads, value_heads, preferred_element_typ...  12.9 us
    unnamed x219, local copies, waits for them, and re-layouts  9.69 us
    unnamed x4, matrix products  9.15 us
  transfers between devices with their start and end apart: 45, of which 24 were waited for; matrix products, arithmetic and copies ran while one was open for 31% of the time, Pallas kernels for 0%

profile of v1, /device:TPU:0, one launch (start us, length us, event | category | flops | bytes accessed | tf_op | source)
XLA Modules:
  0.0 417.6 jit_solution(11979814875888977810)
XLA Ops:
  21.6 10.5 %collective-permute-done = bf16[768,3,192]{0,2,1:T(8,128)(2,1)S(1)} collective-permute-done((bf16[768,3,192]{0,2,1:T(8,128)(2,1)}, bf16[768,3,192]{0,2,1:T(8,128)(2,1)S(1)}, u32[]{:S(2)}, u32[]{:S(2)}) %collective-permute-start) | collective-permute-done | bytes 884768 | tf_op jit(solution)/shard_map/ppermute | solution.py:69
  48.4 26.5 %collective-permute-done.4 = bf16[768,768]{1,0:T(8,128)(2,1)S(1)} collective-permute-done((bf16[768,768]{1,0:T(8,128)(2,1)S(1)}, bf16[768,768]{1,0:T(8,128)(2,1)S(1)}, u32[]{:S(2)}, u32[]{:S(2)}) %collective-permute-start.4) | collective-permute-done | bytes 1179680 | tf_op jit(solution)/shard_map/ppermute | solution.py:69
  75.0 24.5 %collective-permute-done.5 = bf16[768,768]{1,0:T(8,128)(2,1)S(1)} collective-permute-done((bf16[768,768]{1,0:T(8,128)(2,1)S(1)}, bf16[768,768]{1,0:T(8,128)(2,1)S(1)}, u32[]{:S(2)}, u32[]{:S(2)}) %collective-permute-start.5) | collective-permute-done | bytes 1179680 | tf_op jit(solution)/shard_map/ppermute | solution.py:69
  101.1 17.6 %multiply_convert_fusion.2 = (bf16[1024,1536]{1,0:T(8,128)(2,1)S(1)}, f32[1024,1536]{1,0:T(8,128)}, f32[1024,1536]{1,0:T(8,128)}) fusion(f32[1536]{0:T(1024)S(1)} %pad_maximum_fusion.17, bf16[768,1536]{1,0:T(8,128)(2,1)S(1)} %constant_dynamic-update-slice_fusion.2, f32[1024,768]{1,0:T(8,128)S(1)} %get-tuple-element.32, f32[768]{0:T(1024)S(1)} %copy-done.90, ...), kind=kOutput, calls=%fused_computation.20 | convolution fusion | flops 2523660288 | bytes 21254144 | tf_op jit(solution)/shard_map/dot_general | solution.py:126
  143.6 6.5 %convert_reduce_fusion = (f32[1536]{0:T(1024)}, bf16[1024,1536]{1,0:T(8,128)(2,1)}) fusion(f32[1024,1536]{1,0:T(8,128)S(1)} %bitcast.166, bf16[768,1536]{1,0:T(8,128)(2,1)S(1)} %copy-done.46, f32[1024,768]{1,0:T(8,128)S(1)} %get-tuple-element.23, f32[1024,1536]{1,0:T(8,128)S(1)} %bitcast.168, f32[1536]{0:T(1024)S(1)} %copy-done.86), kind=kOutput, calls=%fused_computation.18 | convolution fusion | flops 2443442688 | bytes 21245952 | tf_op jit(solution)/shard_map/dot_general | solution.py:146
  150.1 5.2 %convolution_convert_fusion.1 = bf16[768,1536]{1,0:T(8,128)(2,1)S(1)} fusion(bf16[1024,1536]{1,0:T(8,128)(2,1)} %get-tuple-element.95, f32[1024,768]{1,0:T(8,128)S(1)} %get-tuple-element.32, f32[768]{0:T(1024)S(1)} %copy-done.91, f32[768]{0:T(1024)S(1)} %copy-done.70, f32[1024]{0:T(1024)S(1)} %add_rsqrt_fusion.1, f32[1024]{0:T(1024)S(1)} %broadcast_multiply_fusion.5), kind=kOutput, calls=%fused_computation.39 | convolution fusion | flops 2421030912 | bytes 8665088 | tf_op jit(solution)/shard_map/rd,rf->df/dot_general | solution.py:150
  165.3 20.9 %collective-permute-done.38 = bf16[768,768]{1,0:T(8,128)(2,1)} collective-permute-done((bf16[768,768]{1,0:T(8,128)(2,1)}, bf16[768,768]{1,0:T(8,128)(2,1)}, u32[]{:S(2)}, u32[]{:S(2)}) %collective-permute-start.38) | collective-permute-done | bytes 1179680 | tf_op jit(solution)/shard_map/ppermute | solution.py:69
  190.6 20.2 %collective-permute-done.31 = bf16[768,768]{1,0:T(8,128)(2,1)} collective-permute-done((bf16[768,768]{1,0:T(8,128)(2,1)}, bf16[768,768]{1,0:T(8,128)(2,1)}, u32[]{:S(2)}, u32[]{:S(2)}) %collective-permute-start.31) | collective-permute-done | bytes 1179680 | tf_op jit(solution)/shard_map/ppermute | solution.py:69
  214.8 4.2 %multiply_reduce_fusion.4 = (f32[768]{0:T(1024)}, f32[1024]{0:T(1024)S(1)}, f32[1024]{0:T(1024)S(1)}, f32[768]{0:T(1024)}, f32[1024,768]{1,0:T(8,128)S(1)}) fusion(f32[1024,768]{1,0:T(8,128)S(1)} %get-tuple-element.32, f32[1024]{0:T(1024)S(1)} %copy-done.63, f32[1024]{0:T(1024)S(1)} %copy-done.57, f32[768]{0:T(1024)S(1)} %copy-done.71, ...), kind=kLoop, calls=%fused_computation.47 | loop fusion | flops 10220032 | bytes 12608512 | tf_op jit(solution)/shard_map/reduce_sum | solution.py:153
  225.9 6.8 %multiply_reduce_fusion = (f32[3,1024]{1,0:T(4,128)S(1)}, f32[3,1024,1024]{1,2,0:T(8,128)}) fusion(f32[3,1024,1024]{1,2,0:T(8,128)S(1)} %bitcast.118, f32[3,1024]{1,0:T(4,128)S(1)} %log_add_fusion, bf16[1024,3,64]{0,2,1:T(8,128)(2,1)S(1)} %bitcast.126, f32[1024,3,64]{0,2,1:T(8,128)S(1)} %bitcast.134, f32[3,64]{1,0:T(4,128)S(1)} %copy-done.69), kind=kOutput, calls=%fused_computation.1 | convolution fusion | flops 415626240 | bytes 26370816 | tf_op jit(solution)/shard_map/qhd,khd->hqk/dot_general | solution.py:51
  232.6 10.2 %multiply_convert_fusion = bf16[3,1024,1024]{1,2,0:T(8,128)(2,1)} fusion(f32[3,1024,1024]{1,2,0:T(8,128)} %get-tuple-element.93, f32[3,1024,1024]{1,2,0:T(8,128)S(1)} %bitcast.118, f32[3,1024]{1,0:T(4,128)S(1)} %get-tuple-element.92, f32[3,1024]{1,0:T(4,128)} %copy-done.42), kind=kLoop, calls=%fused_computation | loop fusion | flops 15728640 | bytes 31481856 | tf_op jit(solution)/shard_map/convert_element_type | solution.py:53
  242.8 5.0 %fusion.32 = bf16[3,64,1024]{2,1,0:T(8,128)(2,1)S(1)} fusion(bf16[3,1024,1024]{1,2,0:T(8,128)(2,1)} %multiply_convert_fusion, f32[1024,3,64]{0,2,1:T(8,128)S(1)} %bitcast.122, f32[3,64]{1,0:T(4,128)S(1)} %copy-done.61), kind=kOutput, calls=%fused_computation.96 | convolution fusion | flops 403439616 | bytes 7471872 | tf_op jit(solution)/shard_map/hqk,qhd->khd/dot_general | solution.py:55
  251.5 6.2 %multiply_reduce_fusion.1 = (f32[3,1024]{1,0:T(4,128)S(1)}, f32[3,1024,1024]{1,2,0:T(8,128)}) fusion(f32[3,1024,1024]{1,2,0:T(8,128)S(1)} %bitcast.116, f32[3,1024]{1,0:T(4,128)S(1)} %log_add_fusion.1, bf16[1024,3,64]{0,2,1:T(8,128)(2,1)S(1)} %bitcast.124, f32[1024,3,64]{0,2,1:T(8,128)S(1)} %bitcast.132, f32[3,64]{1,0:T(4,128)S(1)} %copy-done.67), kind=kOutput, calls=%fused_computation.4 | convolution fusion | flops 415626240 | bytes 26370816 | tf_op jit(solution)/shard_map/qhd,khd->hqk/dot_general | solution.py:51
  262.3 9.9 %multiply_convert_fusion.1 = bf16[3,1024,1024]{1,2,0:T(8,128)(2,1)S(1)} fusion(f32[3,1024,1024]{1,2,0:T(8,128)} %get-tuple-element.91, f32[3,1024,1024]{1,2,0:T(8,128)} %copy-done, f32[3,1024]{1,0:T(4,128)S(1)} %get-tuple-element.90, f32[3,1024]{1,0:T(4,128)S(1)} %log_add_fusion.1), kind=kLoop, calls=%fused_computation.3 | loop fusion | flops 15728640 | bytes 31481856 | tf_op jit(solution)/shard_map/convert_element_type | solution.py:53
  317.4 8.4 %collective-permute-done.26 = bf16[192,192]{0,1:T(8,128)(2,1)S(1)} collective-permute-done((bf16[192,192]{0,1:T(8,128)(2,1)S(1)}, bf16[192,192]{0,1:T(8,128)(2,1)S(1)}, u32[]{:S(2)}, u32[]{:S(2)}) %collective-permute-start.26) | collective-permute-done | bytes 73760 | tf_op jit(solution)/shard_map/ppermute | solution.py:69
  334.7 6.0 %collective-permute-done.28 = bf16[96,192]{0,1:T(8,128)(2,1)S(1)} collective-permute-done((bf16[96,192]{0,1:T(8,128)(2,1)S(1)}, bf16[96,192]{0,1:T(8,128)(2,1)S(1)}, u32[]{:S(2)}, u32[]{:S(2)}) %collective-permute-start.28) | collective-permute-done | bytes 36896 | tf_op jit(solution)/shard_map/ppermute | solution.py:69
  347.4 6.1 %collective-permute-done.42 = bf16[96,768]{1,0:T(8,128)(2,1)S(1)} collective-permute-done((bf16[96,768]{1,0:T(8,128)(2,1)S(1)}, bf16[96,768]{1,0:T(8,128)(2,1)S(1)}, u32[]{:S(2)}, u32[]{:S(2)}) %collective-permute-start.42) | collective-permute-done | bytes 147488 | tf_op jit(solution)/shard_map/ppermute | solution.py:69
  358.8 4.8 %collective-permute-done.43 = bf16[192,768]{1,0:T(8,128)(2,1)S(1)} collective-permute-done((bf16[192,768]{1,0:T(8,128)(2,1)S(1)}, bf16[192,768]{1,0:T(8,128)(2,1)S(1)}, u32[]{:S(2)}, u32[]{:S(2)}) %collective-permute-start.43) | collective-permute-done | bytes 294944 | tf_op jit(solution)/shard_map/ppermute | solution.py:69
  364.3 6.2 %collective-permute-done.14 = bf16[384,3,192]{0,2,1:T(8,128)(2,1)S(1)} collective-permute-done((bf16[384,3,192]{0,2,1:T(8,128)(2,1)S(1)}, bf16[384,3,192]{0,2,1:T(8,128)(2,1)S(1)}, u32[]{:S(2)}, u32[]{:S(2)}) %collective-permute-start.14) | collective-permute-done | bytes 442400 | tf_op jit(solution)/shard_map/ppermute | solution.py:69
  373.3 5.5 %collective-permute-done.15 = bf16[192,3,192]{0,2,1:T(8,128)(2,1)S(1)} collective-permute-done((bf16[192,3,192]{0,2,1:T(8,128)(2,1)S(1)}, bf16[192,3,192]{0,2,1:T(8,128)(2,1)S(1)}, u32[]{:S(2)}, u32[]{:S(2)}) %collective-permute-start.15) | collective-permute-done | bytes 221216 | tf_op jit(solution)/shard_map/ppermute | solution.py:69
  382.7 7.1 %collective-permute-done.16 = bf16[96,3,192]{0,2,1:T(8,128)(2,1)S(1)} collective-permute-done((bf16[96,3,192]{0,2,1:T(8,128)(2,1)S(1)}, bf16[96,3,192]{0,2,1:T(8,128)(2,1)S(1)}, u32[]{:S(2)}, u32[]{:S(2)}) %collective-permute-start.16) | collective-permute-done | bytes 110624 | tf_op jit(solution)/shard_map/ppermute | solution.py:69
  391.6 5.5 %collective-permute-done.17 = bf16[96,3,192]{0,2,1:T(8,128)(2,1)S(1)} collective-permute-done((bf16[96,3,192]{0,2,1:T(8,128)(2,1)S(1)}, bf16[96,3,192]{0,2,1:T(8,128)(2,1)S(1)}, u32[]{:S(2)}, u32[]{:S(2)}) %collective-permute-start.17) | collective-permute-done | bytes 110624 | tf_op jit(solution)/shard_map/ppermute | solution.py:69
  397.6 6.5 %collective-permute-done.18 = bf16[192,3,192]{0,2,1:T(8,128)(2,1)S(1)} collective-permute-done((bf16[192,3,192]{0,2,1:T(8,128)(2,1)S(1)}, bf16[192,3,192]{0,2,1:T(8,128)(2,1)S(1)}, u32[]{:S(2)}, u32[]{:S(2)}) %collective-permute-start.18) | collective-permute-done | bytes 221216 | tf_op jit(solution)/shard_map/ppermute | solution.py:69
  408.5 4.4 %collective-permute-done.19 = bf16[384,3,192]{0,2,1:T(8,128)(2,1)S(1)} collective-permute-done((bf16[384,3,192]{0,2,1:T(8,128)(2,1)S(1)}, bf16[384,3,192]{0,2,1:T(8,128)(2,1)S(1)}, u32[]{:S(2)}, u32[]{:S(2)}) %collective-permute-start.19) | collective-permute-done | bytes 442400 | tf_op jit(solution)/shard_map/ppermute | solution.py:69
  (434 shorter events, 179.6 us)
Async XLA Ops:
  1.4 19.8 %collective-permute-start.1 = (f32[1152]{0:T(1024)S(1)}, f32[1152]{0:T(1024)S(1)}, u32[]{:S(2)}, u32[]{:S(2)}) collective-permute-start(f32[1152]{0:T(1024)S(1)} %concatenate.66), channel_id=1, source_target_pairs={{0,2},{1,3},{2,0},{3,1},{4,6},{5,7},{6,4},{7,5},{8,10},{9,11},{10,... | collective-permute-start | bytes 13832 | tf_op jit(solution)/shard_map/ppermute | solution.py:69
  4.4 17.1 %collective-permute-start.2 = (bf16[768,192]{0,1:T(8,128)(2,1)}, bf16[768,192]{0,1:T(8,128)(2,1)S(1)}, u32[]{:S(2)}, u32[]{:S(2)}) collective-permute-start(bf16[768,192]{0,1:T(8,128)(2,1)} %param.21), channel_id=1, source_target_pairs={{0,2},{1,3},{2,0},{3,1},{4,6},{5,7},{6,4},{7,5},{8,10},{9,11},{10,... | collective-permute-start | bytes 884744 | tf_op jit(solution)/shard_map/ppermute | solution.py:69
  4.4 27.6 %collective-permute-start = (bf16[768,3,192]{0,2,1:T(8,128)(2,1)}, bf16[768,3,192]{0,2,1:T(8,128)(2,1)S(1)}, u32[]{:S(2)}, u32[]{:S(2)}) collective-permute-start(bf16[768,3,192]{0,2,1:T(8,128)(2,1)} %param.18), channel_id=1, source_target_pairs={{0,2},{1,3},{2,0},{3,1},{4,6},{5,7},{6,4},{7,5},{8,10},{9,11},{10,... | collective-permute-start | bytes 2654216 | tf_op jit(solution)/shard_map/ppermute | solution.py:69
  45.7 53.8 %collective-permute-start.3 = (bf16[1024,768]{1,0:T(8,128)(2,1)S(1)}, bf16[1024,768]{1,0:T(8,128)(2,1)S(1)}, u32[]{:S(2)}, u32[]{:S(2)}) collective-permute-start(bf16[1024,768]{1,0:T(8,128)(2,1)S(1)} %convolution_convert_fusion.2), channel_id=1, source_target_pairs={{0,1},{1,0},{2,3},{3,2},{4,5},{5,4},{6,7},{7,6},{8,9},{9,8},{10,11... | collective-permute-start | bytes 4718600 | tf_op jit(solution)/shard_map/ppermute | solution.py:69
  46.1 28.8 %collective-permute-start.4 = (bf16[768,768]{1,0:T(8,128)(2,1)S(1)}, bf16[768,768]{1,0:T(8,128)(2,1)S(1)}, u32[]{:S(2)}, u32[]{:S(2)}) collective-permute-start(bf16[768,768]{1,0:T(8,128)(2,1)S(1)} %copy-done.40), channel_id=1, source_target_pairs={{0,2},{1,3},{2,0},{3,1},{4,6},{5,7},{6,4},{7,5},{8,10},{9,11},{10,... | collective-permute-start | bytes 3538952 | tf_op jit(solution)/shard_map/ppermute | solution.py:69
  46.5 53.0 %collective-permute-start.5 = (bf16[768,768]{1,0:T(8,128)(2,1)S(1)}, bf16[768,768]{1,0:T(8,128)(2,1)S(1)}, u32[]{:S(2)}, u32[]{:S(2)}) collective-permute-start(bf16[768,768]{1,0:T(8,128)(2,1)S(1)} %copy-done.41), channel_id=1, source_target_pairs={{0,2},{1,3},{2,0},{3,1},{4,6},{5,7},{6,4},{7,5},{8,10},{9,11},{10,... | collective-permute-start | bytes 3538952 | tf_op jit(solution)/shard_map/ppermute | solution.py:69
  140.3 24.5 %collective-permute-start.7 = (bf16[512,768]{1,0:T(8,128)(2,1)}, bf16[512,768]{1,0:T(8,128)(2,1)}, u32[]{:S(2)}, u32[]{:S(2)}) collective-permute-start(bf16[512,768]{1,0:T(8,128)(2,1)} %constant_dynamic-slice_fusion.13), channel_id=1, source_target_pairs={{0,2},{1,3},{2,0},{3,1},{4,6},{5,7},{6,4},{7,5},{8,10},{9,11},{10,... | collective-permute-start | bytes 2359304 | tf_op jit(solution)/shard_map/ppermute | solution.py:69
  142.0 44.2 %collective-permute-start.38 = (bf16[768,768]{1,0:T(8,128)(2,1)}, bf16[768,768]{1,0:T(8,128)(2,1)}, u32[]{:S(2)}, u32[]{:S(2)}) collective-permute-start(bf16[768,768]{1,0:T(8,128)(2,1)} %slice.97), channel_id=1, source_target_pairs={{0,2},{1,3},{2,0},{3,1},{4,6},{5,7},{6,4},{7,5},{8,10},{9,11},{10,... | collective-permute-start | bytes 3538952 | tf_op jit(solution)/shard_map/ppermute | solution.py:69
  156.6 54.2 %collective-permute-start.31 = (bf16[768,768]{1,0:T(8,128)(2,1)}, bf16[768,768]{1,0:T(8,128)(2,1)}, u32[]{:S(2)}, u32[]{:S(2)}) collective-permute-start(bf16[768,768]{1,0:T(8,128)(2,1)} %slice.95), channel_id=1, source_target_pairs={{0,2},{1,3},{2,0},{3,1},{4,6},{5,7},{6,4},{7,5},{8,10},{9,11},{10,... | collective-permute-start | bytes 3538952 | tf_op jit(solution)/shard_map/ppermute | solution.py:69
  160.8 53.9 %collective-permute-start.9 = (bf16[1024,768]{1,0:T(8,128)(2,1)}, bf16[1024,768]{1,0:T(8,128)(2,1)}, u32[]{:S(2)}, u32[]{:S(2)}) collective-permute-start(bf16[1024,768]{1,0:T(8,128)(2,1)} %convolution_convert_fusion.3), channel_id=1, source_target_pairs={{0,1},{1,0},{2,3},{3,2},{4,5},{5,4},{6,7},{7,6},{8,9},{9,8},{10,11... | collective-permute-start | bytes 4718600 | tf_op jit(solution)/shard_map/ppermute | solution.py:69
  164.8 115.4 %collective-permute-start.8 = (bf16[512,768]{1,0:T(8,128)(2,1)}, bf16[512,768]{1,0:T(8,128)(2,1)}, u32[]{:S(2)}, u32[]{:S(2)}) collective-permute-start(bf16[512,768]{1,0:T(8,128)(2,1)} %collective-permute-done.7), channel_id=1, source_target_pairs={{0,1},{1,0},{2,3},{3,2},{4,5},{5,4},{6,7},{7,6},{8,9},{9,8},{10,11... | collective-permute-start | bytes 2359304 | tf_op jit(solution)/shard_map/ppermute | solution.py:69
  189.1 114.4 %collective-permute-start.39 = (bf16[384,768]{1,0:T(8,128)(2,1)}, bf16[384,768]{1,0:T(8,128)(2,1)}, u32[]{:S(2)}, u32[]{:S(2)}) collective-permute-start(bf16[384,768]{1,0:T(8,128)(2,1)} %constant_dynamic-slice_fusion.2), channel_id=1, source_target_pairs={{0,4},{1,5},{2,6},{3,7},{4,0},{5,1},{6,2},{7,3},{8,12},{9,13},{10,... | collective-permute-start | bytes 1769480 | tf_op jit(solution)/shard_map/ppermute | solution.py:69
  213.2 94.4 %collective-permute-start.32 = (bf16[384,768]{1,0:T(8,128)(2,1)}, bf16[384,768]{1,0:T(8,128)(2,1)}, u32[]{:S(2)}, u32[]{:S(2)}) collective-permute-start(bf16[384,768]{1,0:T(8,128)(2,1)} %constant_dynamic-slice_fusion.5), channel_id=1, source_target_pairs={{0,4},{1,5},{2,6},{3,7},{4,0},{5,1},{6,2},{7,3},{8,12},{9,13},{10,... | collective-permute-start | bytes 1769480 | tf_op jit(solution)/shard_map/ppermute | solution.py:69
  258.4 47.6 %collective-permute-start.24 = (bf16[768,192]{0,1:T(8,128)(2,1)}, bf16[768,192]{0,1:T(8,128)(2,1)}, u32[]{:S(2)}, u32[]{:S(2)}) collective-permute-start(bf16[768,192]{0,1:T(8,128)(2,1)} %slice.93), channel_id=1, source_target_pairs={{0,2},{1,3},{2,0},{3,1},{4,6},{5,7},{6,4},{7,5},{8,10},{9,11},{10,... | collective-permute-start | bytes 884744 | tf_op jit(solution)/shard_map/ppermute | solution.py:69
  260.7 28.0 %collective-permute-start.20 = (f32[5760]{0:T(1024)}, f32[5760]{0:T(1024)}, u32[]{:S(2)}, u32[]{:S(2)}) collective-permute-start(f32[5760]{0:T(1024)} %concatenate.78), channel_id=1, source_target_pairs={{0,2},{1,3},{2,0},{3,1},{4,6},{5,7},{6,4},{7,5},{8,10},{9,11},{10,... | collective-permute-start | bytes 69128 | tf_op jit(solution)/shard_map/ppermute | solution.py:69
  280.2 75.7 %collective-permute-start.13 = (bf16[768,3,192]{0,2,1:T(8,128)(2,1)}, bf16[768,3,192]{0,2,1:T(8,128)(2,1)}, u32[]{:S(2)}, u32[]{:S(2)}) collective-permute-start(bf16[768,3,192]{0,2,1:T(8,128)(2,1)} %convert_element_type.373), channel_id=1, source_target_pairs={{0,2},{1,3},{2,0},{3,1},{4,6},{5,7},{6,4},{7,5},{8,10},{9,11},{10,... | collective-permute-start | bytes 2654216 | tf_op jit(solution)/shard_map/ppermute | solution.py:69
  302.2 80.1 %collective-permute-start.10 = (bf16[1024,768]{1,0:T(8,128)(2,1)S(1)}, bf16[1024,768]{1,0:T(8,128)(2,1)S(1)}, u32[]{:S(2)}, u32[]{:S(2)}) collective-permute-start(bf16[1024,768]{1,0:T(8,128)(2,1)S(1)} %copy-done.37), channel_id=1, source_target_pairs={{0,1},{1,0},{2,3},{3,2},{4,5},{5,4},{6,7},{7,6},{8,9},{9,8},{10,11... | collective-permute-start | bytes 4718600 | tf_op jit(solution)/shard_map/ppermute | solution.py:69
  308.9 18.5 %collective-permute-start.33 = (bf16[192,768]{1,0:T(8,128)(2,1)S(1)}, bf16[192,768]{1,0:T(8,128)(2,1)S(1)}, u32[]{:S(2)}, u32[]{:S(2)}) collective-permute-start(bf16[192,768]{1,0:T(8,128)(2,1)S(1)} %constant_dynamic-slice_fusion.4), channel_id=1, source_target_pairs={{0,8},{1,9},{2,10},{3,11},{4,12},{5,13},{6,14},{7,15},{8,0},{9,1},... | collective-permute-start | bytes 884744 | tf_op jit(solution)/shard_map/ppermute | solution.py:69
  314.7 26.3 %collective-permute-start.41 = (bf16[96,768]{1,0:T(8,128)(2,1)S(1)}, bf16[96,768]{1,0:T(8,128)(2,1)S(1)}, u32[]{:S(2)}, u32[]{:S(2)}) collective-permute-start(bf16[96,768]{1,0:T(8,128)(2,1)S(1)} %constant_dynamic-slice_fusion), channel_id=1, source_target_pairs={{0,16},{1,17},{2,18},{3,19},{4,20},{5,21},{6,22},{7,23},{8,24},{9,... | collective-permute-start | bytes 442376 | tf_op jit(solution)/shard_map/ppermute | solution.py:69
  355.1 17.4 %collective-permute-start.36 = (bf16[192,768]{1,0:T(8,128)(2,1)S(1)}, bf16[192,768]{1,0:T(8,128)(2,1)S(1)}, u32[]{:S(2)}, u32[]{:S(2)}) collective-permute-start(bf16[192,768]{1,0:T(8,128)(2,1)S(1)} %pad_maximum_fusion.13), channel_id=1, source_target_pairs={{0,8},{1,9},{2,10},{3,11},{4,12},{5,13},{6,14},{7,15},{8,0},{9,1},... | collective-permute-start | bytes 884744 | tf_op jit(solution)/shard_map/ppermute | solution.py:69
  357.3 13.2 %collective-permute-start.14 = (bf16[384,3,192]{0,2,1:T(8,128)(2,1)S(1)}, bf16[384,3,192]{0,2,1:T(8,128)(2,1)S(1)}, u32[]{:S(2)}, u32[]{:S(2)}) collective-permute-start(bf16[384,3,192]{0,2,1:T(8,128)(2,1)S(1)} %constant_dynamic-slice_fusion.11), channel_id=1, source_target_pairs={{0,4},{1,5},{2,6},{3,7},{4,0},{5,1},{6,2},{7,3},{8,12},{9,13},{10,... | collective-permute-start | bytes 1327112 | tf_op jit(solution)/shard_map/ppermute | solution.py:69
  363.7 33.7 %collective-permute-start.44 = (bf16[384,768]{1,0:T(8,128)(2,1)S(1)}, bf16[384,768]{1,0:T(8,128)(2,1)S(1)}, u32[]{:S(2)}, u32[]{:S(2)}) collective-permute-start(bf16[384,768]{1,0:T(8,128)(2,1)S(1)} %pad_maximum_fusion.8), channel_id=1, source_target_pairs={{0,4},{1,5},{2,6},{3,7},{4,0},{5,1},{6,2},{7,3},{8,12},{9,13},{10,... | collective-permute-start | bytes 1769480 | tf_op jit(solution)/shard_map/ppermute | solution.py:69
  372.7 32.4 %collective-permute-start.37 = (bf16[384,768]{1,0:T(8,128)(2,1)S(1)}, bf16[384,768]{1,0:T(8,128)(2,1)S(1)}, u32[]{:S(2)}, u32[]{:S(2)}) collective-permute-start(bf16[384,768]{1,0:T(8,128)(2,1)S(1)} %pad_maximum_fusion.7), channel_id=1, source_target_pairs={{0,4},{1,5},{2,6},{3,7},{4,0},{5,1},{6,2},{7,3},{8,12},{9,13},{10,... | collective-permute-start | bytes 1769480 | tf_op jit(solution)/shard_map/ppermute | solution.py:69
  390.1 15.0 %collective-permute-start.11 = (bf16[512,768]{1,0:T(8,128)(2,1)S(1)}, bf16[512,768]{1,0:T(8,128)(2,1)S(1)}, u32[]{:S(2)}, u32[]{:S(2)}) collective-permute-start(bf16[512,768]{1,0:T(8,128)(2,1)S(1)} %constant_dynamic-slice_fusion.12), channel_id=1, source_target_pairs={{0,2},{1,3},{2,0},{3,1},{4,6},{5,7},{6,4},{7,5},{8,10},{9,11},{10,... | collective-permute-start | bytes 2359304 | tf_op jit(solution)/shard_map/ppermute | solution.py:69
  (129 other events, 1272.1 us)
